TPU v7x, 256 devices: a whole 4x4x8 slice. The times are simulated.
256 devices in a mesh: expert: 64 (over z, y, core), dp: 4 (over x).
Axes of the slice: x: 4, y: 4, z: 8, core: 2. Of those that a mesh axis runs over, the one named last changes fastest.
Arguments:
- tokens: bfloat16 [4, 8192, 2048], P('dp', 'expert'), may hold values from -6 to 6
- cotangent: bfloat16 [4, 8192, 2048], P('dp', 'expert'), may hold values from -6 to 6
- picks: int32 [4, 64, 256], P('dp', 'expert'), may hold values from 0 to 8191, as said below
- valid: int32 [4, 64, 256], P('dp', 'expert'), may hold values 0 or 1
- comb: float32 [4, 64, 256], P('dp', 'expert'), may hold values from 0.25 to 1
- w_in: bfloat16 [64, 2048, 1024], P('expert'), may hold values from -0.125 to 0.125
- w_out: bfloat16 [64, 1024, 2048], P('expert'), may hold values from -0.1875 to 0.1875
Outputs:
- mixed: bfloat16 [4, 8192, 2048], P('dp', 'expert')
- grad_tokens: bfloat16 [4, 8192, 2048], P('dp', 'expert')
- grad_in: bfloat16 [64, 2048, 1024], P('expert', 'dp')
- grad_out: bfloat16 [64, 1024, 2048], P('expert', None, 'dp')
Inputs may be any that keep to these rules, and one draw needn't show every extreme that they name: `picks`: each slot names a token of its group; the 256 slots of one expert in one group name distinct tokens, and at most 8 of them name tokens of one device's 128; for every expert and group some device's tokens are named by exactly 8 slots. Padded slots name tokens like the others.
All inputs are finite; a program needn't handle non-finite values. No bound on the sum of `valid` on one device may be relied on, other than what follows from the above.
Results may differ from a plain program's by a relative error of at most 0.013.
Values may be sent and summed in bfloat16 or wider, within the bound.
A program may use at most 128 MiB of HBM per device.

v0:
```python
from functools import partial

import jax
import jax.numpy as jnp
from jax import lax
from jax.sharding import PartitionSpec as P


def gelu_pair(pre_act):
    return jax.vjp(partial(jax.nn.gelu, approximate=True), pre_act)


def body(tokens, cotangent, picks, valid, comb, w_in, w_out):
    n_expert = lax.axis_size("expert")
    tok_dev = tokens.shape[1]
    model_width = tokens.shape[2]
    exp_dev = picks.shape[1]
    capacity = picks.shape[2]
    most_slots = max(2, 2 * capacity // n_expert)
    slot_width = exp_dev * most_slots
    own_picks = picks[0]
    owner_dev = own_picks // tok_dev
    local_row = own_picks % tok_dev
    owner_hot = (
        owner_dev[:, :, None] == jnp.arange(n_expert, dtype=jnp.int32)[None, None, :]
    ).astype(jnp.int32)
    earlier = jnp.cumsum(owner_hot, axis=1) - owner_hot
    slot_rank = jnp.sum(earlier * owner_hot, axis=2)
    slot_index = (
        owner_dev * slot_width
        + jnp.arange(exp_dev, dtype=jnp.int32)[:, None] * most_slots
        + slot_rank
    )
    slot_flat = slot_index.reshape(-1)
    requests = (
        jnp.zeros((n_expert * slot_width,), jnp.int32).at[slot_flat].set(local_row.reshape(-1))
    )
    asked = lax.all_to_all(
        requests.reshape(n_expert, slot_width), "expert", split_axis=0, concat_axis=0, tiled=True
    )
    asked_flat = asked.reshape(-1)

    def pull(source):
        return jnp.take(source[0], asked_flat, axis=0).reshape(n_expert, slot_width, model_width)

    def compact(received):
        return jnp.take(received.reshape(-1, model_width), slot_flat, axis=0).reshape(
            exp_dev, capacity, model_width
        )

    def place(slot_rows):
        buffer = jnp.zeros((n_expert * slot_width, model_width), jnp.bfloat16)
        return (
            buffer.at[slot_flat]
            .set(slot_rows.reshape(-1, model_width))
            .reshape(n_expert, slot_width, model_width)
        )

    def spread(received):
        total = jnp.zeros((tok_dev, model_width), jnp.float32)
        total = total.at[asked_flat].add(received.reshape(-1, model_width).astype(jnp.float32))
        return total.astype(jnp.bfloat16)[None]

    got_tokens = lax.all_to_all(pull(tokens), "expert", split_axis=0, concat_axis=0, tiled=True)
    token_in = compact(got_tokens)
    slot_scale = (comb[0] * valid[0].astype(jnp.float32))[:, :, None]
    pre_act = jnp.einsum("kcd,kdf->kcf", token_in, w_in, preferred_element_type=jnp.float32)
    act_value, act_back = gelu_pair(pre_act)
    hidden = act_value.astype(jnp.bfloat16)
    expert_out = jnp.einsum("kcf,kfd->kcd", hidden, w_out, preferred_element_type=jnp.float32)
    contrib = (slot_scale * expert_out).astype(jnp.bfloat16)
    mixed = spread(
        lax.all_to_all(place(contrib), "expert", split_axis=0, concat_axis=0, tiled=True)
    )
    got_cot = lax.all_to_all(pull(cotangent), "expert", split_axis=0, concat_axis=0, tiled=True)
    cot_in = compact(got_cot)
    d_out = (slot_scale * cot_in.astype(jnp.float32)).astype(jnp.bfloat16)
    d_hidden = jnp.einsum("kcd,kfd->kcf", d_out, w_out, preferred_element_type=jnp.float32)
    d_pre = act_back(d_hidden)[0].astype(jnp.bfloat16)
    d_token = jnp.einsum("kcf,kdf->kcd", d_pre, w_in, preferred_element_type=jnp.float32).astype(
        jnp.bfloat16
    )
    grad_tokens = spread(
        lax.all_to_all(place(d_token), "expert", split_axis=0, concat_axis=0, tiled=True)
    )
    local_in = jnp.einsum(
        "kcd,kcf->kdf", token_in, d_pre, preferred_element_type=jnp.float32
    ).astype(jnp.bfloat16)
    local_out = jnp.einsum(
        "kcf,kcd->kfd", hidden, d_out, preferred_element_type=jnp.float32
    ).astype(jnp.bfloat16)
    summed_in, summed_out = (
        lax.psum_scatter(local_in, "dp", scatter_dimension=1, tiled=True).astype(jnp.float32),
        lax.psum_scatter(local_out, "dp", scatter_dimension=2, tiled=True).astype(jnp.float32),
    )
    grad_in = summed_in.astype(jnp.bfloat16)
    grad_out = summed_out.astype(jnp.bfloat16)
    return (mixed, grad_tokens, grad_in, grad_out)


def solution(mesh):
    placed = (
        P("dp", "expert", None),
        P("dp", "expert", None),
        P("dp", "expert", None),
        P("dp", "expert", None),
        P("dp", "expert", None),
        P("expert", None, None),
        P("expert", None, None),
    )
    return jax.shard_map(
        body,
        mesh=mesh,
        in_specs=placed,
        out_specs=(
            P("dp", "expert", None),
            P("dp", "expert", None),
            P("expert", "dp", None),
            P("expert", None, "dp"),
        ),
        check_vma=False,
    )
```

profile of v0, /device:TPU:6, one launch (start us, length us, event | category | flops | bytes accessed | tf_op | source)
XLA Modules:
  0.0 304.7 jit_solution(3328673506144791916)
XLA Ops:
  7.2 0.0 copy-start
  7.2 0.7 and_select_fusion.1
  7.9 0.1 compare_convert_fusion
  8.0 0.6 reduce-window.6
  8.6 0.2 slice_reduce_fusion
  8.8 0.1 copy.15
  8.9 0.1 copy.16
  9.0 0.1 broadcast.260
  9.1 0.1 fusion.38
  9.3 0.7 compare_select_fusion.2
  10.0 1.4 scatter_custom_fusion
  11.4 0.1 all_to_all.18
  11.5 21.5 %all_to_all.29 = s32[64,1,8]{2,1,0:T(1,128)S(1)} all-to-all(s32[64,1,8]{2,1,0:T(1,128)S(1)} %bitcast.91), channel_id=1, replica_groups=mesh['expert'=64,'dp'=4] {'expert'}, dimensions={0} | all-to-all | bytes 4096 | tf_op jit(solution)/shard_map/all_to_all | solution.py:38
  33.0 0.1 reshape.462
  33.1 0.0 copy-done
  33.1 0.0 copy-start.1
  33.1 2.5 gather_fusion
  35.6 0.0 copy-done.1
  35.6 3.3 %gather_fusion.2 = bf16[512,2048]{1,0:T(8,128)(2,1)} fusion(bf16[128,2048]{1,0:T(8,128)(2,1)S(1)} %bitcast.82, s32[1024]{0:T(1024)S(1)} %pad_clamp_fusion.1), kind=kCustom, calls=%fused_computation.2.clone | custom fusion | bytes 4196352 | tf_op jit(solution)/shard_map/jit(_take)/gather | solution.py:44
  38.9 3.4 %select_bitcast_fusion = (bf16[64,8,2048]{2,1,0:T(8,128)(2,1)}, bf16[64,8,2048]{2,1,0:T(8,128)(2,1)S(1)}) fusion(bf16[512,2048]{1,0:T(8,128)(2,1)} %gather_fusion.2, pred[512]{0:T(512)(128)(4,1)S(1)} %compare_and_fusion.1, bf16[512,2048]{1,0:T(8,128)(2,1)S(1)} %gather_fusion), kind=kLoop, calls=%fused_computation.28 | loop fusion | flops 2097152 | bytes 8389120 | tf_op jit(solution)/shard_map/reshape | solution.py:44
  42.3 55.8 %all_to_all.30 = bf16[64,8,2048]{2,1,0:T(8,128)(2,1)} all-to-all(bf16[64,8,2048]{2,1,0:T(8,128)(2,1)S(1)} %get-tuple-element.11), channel_id=1, replica_groups=mesh['expert'=64,'dp'=4] {'expert'}, dimensions={0} | all-to-all | bytes 4194304 | tf_op jit(solution)/shard_map/all_to_all | solution.py:64
  98.1 0.0 copy-start.5
  98.1 0.0 copy-start.6
  98.1 5.5 %all-to-all-start.3 = ((bf16[64,8,2048]{2,1,0:T(8,128)(2,1)}), bf16[64,8,2048]{2,1,0:T(8,128)(2,1)S(1)}, u32[]{:S(2)}, u32[]{:S(2)}) async-start(bf16[64,8,2048]{2,1,0:T(8,128)(2,1)} %get-tuple-element.10), calls=%async_computation.3 | async-start | bytes 4194304 | tf_op jit(solution)/shard_map/all_to_all | solution.py:75
  103.6 0.3 reduce-scatter.3.cloned.1.call-start
  104.0 0.0 copy-done.5
  104.0 0.0 copy-done.6
  104.0 5.2 %gather_fusion.1 = bf16[256,2048]{1,0:T(8,128)(2,1)} fusion(bf16[512,2048]{1,0:T(8,128)(2,1)} %bitcast.84, s32[1024]{0:T(1024)S(1)} %pad_clamp_fusion), kind=kCustom, calls=%fused_computation.1.clone | custom fusion | bytes 2098176 | tf_op jit(solution)/shard_map/jit(_take)/gather | solution.py:47
  109.2 45.8 %all-to-all-done.3 = bf16[64,8,2048]{2,1,0:T(8,128)(2,1)S(1)} async-done(((bf16[64,8,2048]{2,1,0:T(8,128)(2,1)}), bf16[64,8,2048]{2,1,0:T(8,128)(2,1)S(1)}, u32[]{:S(2)}, u32[]{:S(2)}) %all-to-all-start.3) | async-done | bytes 2097184 | tf_op jit(solution)/shard_map/all_to_all | solution.py:75
  155.0 2.3 gather_fusion.3
  157.3 0.0 copy-start.3
  157.3 0.0 copy-start.7
  157.3 3.9 %fusion.10 = f32[256,1024]{1,0:T(8,128)S(1)} fusion(bf16[1,2048,1024]{2,1,0:T(8,128)(2,1)} %param.16, bf16[256,2048]{1,0:T(8,128)(2,1)} %gather_fusion.1, pred[256]{0:T(512)(128)(4,1)S(1)} %get-tuple-element.6), kind=kOutput, calls=%fused_computation.19 | convolution fusion | flops 1074266112 | bytes 6291712 | tf_op jit(solution)/shard_map/kcd,kdf->kcf/dot_general | solution.py:67
  161.2 0.0 copy-start.8
  161.3 0.0 copy-done.3
  161.3 0.1 copy-done.7
  161.4 0.0 copy-start.4
  161.4 1.8 fusion.29
  163.2 0.0 copy-done.8
  163.2 0.0 copy-done.4
  163.2 3.3 %convert_bitcast_fusion.1 = bf16[1,2048,1024]{2,1,0:T(8,128)(2,1)} fusion(bf16[256,1024]{1,0:T(8,128)(2,1)S(1)} %fusion.29, bf16[256,2048]{1,0:T(8,128)(2,1)S(1)} %copy-done.4, pred[256]{0:T(512)(128)(4,1)S(1)} %get-tuple-element.6), kind=kOutput, calls=%fused_computation.22 | convolution fusion | flops 1076363264 | bytes 5767424 | tf_op jit(solution)/shard_map/kcd,kcf->kdf/dot_general | solution.py:86
  166.5 0.0 reduce-scatter.3.cloned.1.call-update
  166.5 3.5 %fusion.18 = bf16[256,2048]{1,0:T(8,128)(2,1)S(1)} fusion(bf16[256,1024]{1,0:T(8,128)(2,1)S(1)} %fusion.29, bf16[1,2048,1024]{2,1,0:T(8,128)(2,1)} %param.16), kind=kOutput, calls=%fused_computation.25 | convolution fusion | flops 1074266112 | bytes 5767168 | tf_op jit(solution)/shard_map/kcf,kdf->kcd/dot_general | solution.py:80
  170.0 3.8 %scatter_custom_fusion.3 = bf16[512,2048]{1,0:T(8,128)(2,1)} fusion(s32[256]{0:T(256)S(1)} %bitcast.98, bf16[256,2048]{1,0:T(8,128)(2,1)S(1)} %fusion.18, bf16[]{:T(256)} %constant.69.clone.1), kind=kCustom, calls=%fused_computation.41 | custom fusion | bytes 2097154 | tf_op jit(solution)/shard_map/scatter | solution.py:55
  173.8 5.4 %all-to-all-start.4 = ((bf16[64,8,2048]{2,1,0:T(8,128)(2,1)}), bf16[64,8,2048]{2,1,0:T(8,128)(2,1)S(1)}, u32[]{:S(2)}, u32[]{:S(2)}) async-start(bf16[64,8,2048]{2,1,0:T(8,128)(2,1)} %bitcast.85), calls=%async_computation.4 | async-start | bytes 4194304 | tf_op jit(solution)/shard_map/all_to_all | solution.py:84
  179.2 0.6 reduce-scatter.5.cloned.1.call-start
  179.7 5.1 %convert_bitcast_fusion = bf16[1,1024,2048]{2,1,0:T(8,128)(2,1)} fusion(bf16[256,2048]{1,0:T(8,128)(2,1)} %gather_fusion.3, f32[256]{0:T(256)S(1)} %bitcast.101, pred[256]{0:T(512)(128)(4,1)S(1)} %get-tuple-element.6, f32[256,1024]{1,0:T(8,128)} %copy-done.8), kind=kOutput, calls=%fused_computation.21 | convolution fusion | flops 1080295424 | bytes 6292736 | tf_op jit(solution)/shard_map/kcf,kcd->kfd/dot_general | solution.py:89
  184.9 0.0 reduce-scatter.5.cloned.1.call-update
  184.9 5.0 %fusion.15 = bf16[256,2048]{1,0:T(8,128)(2,1)} fusion(bf16[1,1024,2048]{2,1,0:T(8,128)(2,1)} %param.17, f32[256]{0:T(256)S(1)} %bitcast.102, f32[256,1024]{1,0:T(8,128)} %copy-done.8), kind=kOutput, calls=%fused_computation.24 | convolution fusion | flops 1077149696 | bytes 6292480 | tf_op jit(solution)/shard_map/kcf,kfd->kcd/dot_general | solution.py:70
  189.9 4.4 %scatter_custom_fusion.1 = bf16[512,2048]{1,0:T(8,128)(2,1)} fusion(s32[256]{0:T(256)S(1)} %bitcast.99, bf16[256,2048]{1,0:T(8,128)(2,1)} %fusion.15, bf16[]{:T(256)} %constant.69.clone.1), kind=kCustom, calls=%fused_computation.43 | custom fusion | bytes 2097664 | tf_op jit(solution)/shard_map/scatter | solution.py:55
  194.3 36.3 %all-to-all-done.4 = bf16[64,8,2048]{2,1,0:T(8,128)(2,1)S(1)} async-done(((bf16[64,8,2048]{2,1,0:T(8,128)(2,1)}), bf16[64,8,2048]{2,1,0:T(8,128)(2,1)S(1)}, u32[]{:S(2)}, u32[]{:S(2)}) %all-to-all-start.4) | async-done | bytes 2097184 | tf_op jit(solution)/shard_map/all_to_all | solution.py:84
  230.5 5.8 %all-to-all-start.2 = ((bf16[64,8,2048]{2,1,0:T(8,128)(2,1)}), bf16[64,8,2048]{2,1,0:T(8,128)(2,1)}, u32[]{:S(2)}, u32[]{:S(2)}) async-start(bf16[64,8,2048]{2,1,0:T(8,128)(2,1)} %bitcast.86), calls=%async_computation.2 | async-start | bytes 4194304 | tf_op jit(solution)/shard_map/all_to_all | solution.py:73
  236.3 0.5 broadcast.346
  236.8 0.7 reduce.8
  237.6 0.1 reshape.461
  237.7 8.3 %scatter_custom_fusion.4 = f32[128,2048]{1,0:T(8,128)} fusion(s32[512]{0:T(512)S(1)} %bitcast.95, bf16[64,8,2048]{2,1,0:T(8,128)(2,1)S(1)} %all-to-all-done.4, f32[]{:T(128)} %constant.40.clone.1), kind=kCustom, calls=%fused_computation.9 | custom fusion | flops 2097152 | bytes 3145732 | tf_op jit(solution)/shard_map/scatter-add | solution.py:61
  246.0 0.0 copy-start.2
  246.0 41.5 %all-to-all-done.2 = bf16[64,8,2048]{2,1,0:T(8,128)(2,1)} async-done(((bf16[64,8,2048]{2,1,0:T(8,128)(2,1)}), bf16[64,8,2048]{2,1,0:T(8,128)(2,1)}, u32[]{:S(2)}, u32[]{:S(2)}) %all-to-all-start.2) | async-done | bytes 2097184 | tf_op jit(solution)/shard_map/all_to_all | solution.py:73
  287.5 8.4 %scatter_custom_fusion.2 = f32[128,2048]{1,0:T(8,128)S(1)} fusion(s32[512]{0:T(512)S(1)} %bitcast.96, bf16[64,8,2048]{2,1,0:T(8,128)(2,1)} %all-to-all-done.2, f32[]{:T(128)} %constant.40.clone.1), kind=kCustom, calls=%fused_computation.11 | custom fusion | flops 2097152 | bytes 3145732 | tf_op jit(solution)/shard_map/scatter-add | solution.py:61
  295.9 0.0 copy-done.2
  295.9 0.9 convert_bitcast_fusion.2
  296.7 0.9 convert_bitcast_fusion.3
  297.6 0.0 reduce-scatter.3.cloned.1.call-done
  297.6 0.0 reduce-scatter.5.cloned.1.call-done
  (10 shorter events, 0.1 us)
Async XLA Ops:
  7.2 25.9 %copy-start = (bf16[1,128,2048]{2,1,0:T(8,128)(2,1)S(1)}, bf16[1,128,2048]{2,1,0:T(8,128)(2,1)}, u32[]{:S(2)}) copy-start(bf16[1,128,2048]{2,1,0:T(8,128)(2,1)} %param.11) | copy-start | bytes 1572868
  33.1 2.5 copy-start.1
  98.1 5.9 %copy-start.5 = (f32[1,1,256]{2,1,0:T(1,128)S(1)}, f32[1,1,256]{2,1,0:T(1,128)}, u32[]{:S(2)}) copy-start(f32[1,1,256]{2,1,0:T(1,128)} %param.15) | copy-start | bytes 3076
  98.1 5.9 %copy-start.6 = (s32[1,1,256]{2,1,0:T(1,128)S(1)}, s32[1,1,256]{2,1,0:T(1,128)}, u32[]{:S(2)}) copy-start(s32[1,1,256]{2,1,0:T(1,128)} %param.14) | copy-start | bytes 3076
  98.1 56.8 %all-to-all-start.3 = ((bf16[64,8,2048]{2,1,0:T(8,128)(2,1)}), bf16[64,8,2048]{2,1,0:T(8,128)(2,1)S(1)}, u32[]{:S(2)}, u32[]{:S(2)}) async-start(bf16[64,8,2048]{2,1,0:T(8,128)(2,1)} %get-tuple-element.10), calls=%async_computation.3 | async-start | bytes 4194304 | tf_op jit(solution)/shard_map/all_to_all | solution.py:75
  103.6 194.0 %reduce-scatter.3.cloned.1.call-start = ((), (), s32[]{:S(2)}) async-start(), calls=%async_computation.7 | async-start | bytes 5242880 | tf_op jit(solution)/shard_map/reduce_scatter | solution.py:93
  157.3 4.0 %copy-start.3 = (bf16[256,2048]{1,0:T(8,128)(2,1)S(1)}, bf16[256,2048]{1,0:T(8,128)(2,1)}, u32[]{:S(2)}) copy-start(bf16[256,2048]{1,0:T(8,128)(2,1)} %gather_fusion.3) | copy-start | bytes 3145732
  157.3 4.1 %copy-start.7 = (bf16[1,1024,2048]{2,1,0:T(8,128)(2,1)S(1)}, bf16[1,1024,2048]{2,1,0:T(8,128)(2,1)}, u32[]{:S(2)}) copy-start(bf16[1,1024,2048]{2,1,0:T(8,128)(2,1)} %param.17) | copy-start | bytes 12582916
  161.2 1.9 copy-start.8
  161.4 1.8 copy-start.4
  173.8 56.7 %all-to-all-start.4 = ((bf16[64,8,2048]{2,1,0:T(8,128)(2,1)}), bf16[64,8,2048]{2,1,0:T(8,128)(2,1)S(1)}, u32[]{:S(2)}, u32[]{:S(2)}) async-start(bf16[64,8,2048]{2,1,0:T(8,128)(2,1)} %bitcast.85), calls=%async_computation.4 | async-start | bytes 4194304 | tf_op jit(solution)/shard_map/all_to_all | solution.py:84
  179.2 118.4 %reduce-scatter.5.cloned.1.call-start = ((), (), s32[]{:S(2)}) async-start(), calls=%async_computation.8 | async-start | bytes 5242880 | tf_op jit(solution)/shard_map/reduce_scatter | solution.py:94
  230.5 57.0 %all-to-all-start.2 = ((bf16[64,8,2048]{2,1,0:T(8,128)(2,1)}), bf16[64,8,2048]{2,1,0:T(8,128)(2,1)}, u32[]{:S(2)}, u32[]{:S(2)}) async-start(bf16[64,8,2048]{2,1,0:T(8,128)(2,1)} %bitcast.86), calls=%async_computation.2 | async-start | bytes 4194304 | tf_op jit(solution)/shard_map/all_to_all | solution.py:73
  246.0 49.9 %copy-start.2 = (f32[128,2048]{1,0:T(8,128)S(1)}, f32[128,2048]{1,0:T(8,128)}, u32[]{:S(2)}) copy-start(f32[128,2048]{1,0:T(8,128)} %scatter_custom_fusion.4) | copy-start | bytes 3145732
Sparse Core Ops, SparseCore 0:
  166.6 43.6 reduce-scatter.2
  213.6 49.0 reduce-scatter.4
where the time goes:
time: 311 us; the launch traced here: 305 us
  waiting for transfers between devices  124 us (40%)
  blocking collectives  77.4 us (25%)
  other arithmetic  24.9 us (8%)
  local copies, waits for them, and re-layouts  24.2 us (8%)
  matrix products  22.6 us (7%)
  starting transfers between devices  17.5 us (6%)
  between operations  14.5 us (5%)
    all_to_all x1, blocking collectives, body(): lax.all_to_all(pull(tokens), 'expert', split_axis=0, concat_axis=0, tiled...  55.8 us
    all_to_all x1, waiting for transfers between devices, body(): lax.all_to_all(pull(cotangent), 'expert', split_axis=0, concat_axis=0, ti...  45.8 us
    all_to_all x1, waiting for transfers between devices, body(): lax.all_to_all(place(contrib), 'expert', split_axis=0, concat_axis=0, til...  41.5 us
    all_to_all x1, waiting for transfers between devices, body(): lax.all_to_all(place(d_token), 'expert', split_axis=0, concat_axis=0, til...  36.3 us
    all_to_all x1, blocking collectives, body(): lax.all_to_all(requests.reshape(n_expert, slot_width), 'expert', split_ax...  21.5 us
    scatter-add x2, other arithmetic, spread(): total.at[asked_flat]  16.7 us
    scatter x2, local copies, waits for them, and re-layouts, place(): return buffer.at[slot_flat].set(slot_rows.reshape(-1, model_width)).resha...  8.16 us
    gather x2, local copies, waits for them, and re-layouts, compact(): jnp.take(received.reshape(-1, model_width), slot_flat, axis=0)  7.52 us
  transfers between devices with their start and end apart: 5, of which 3 were waited for; matrix products, arithmetic and copies ran while one was open for 15% of the time, Pallas kernels for 0%

commit v1 on v0

v1 whole, which is shorter than its diff:
```python
from functools import partial

import jax
import jax.numpy as jnp
from jax import lax
from jax.experimental import pallas as pl
from jax.experimental.pallas import tpu as pltpu
from jax.sharding import PartitionSpec as P

MESH = pl.DeviceIdType.MESH
PLANE = 8
MOST = 8
TIGHT = 304
VMEM = pl.BlockSpec(memory_space=pltpu.VMEM)
BF = jnp.bfloat16
F32 = jnp.float32
I32 = jnp.int32


def dot(a, b):
    return jnp.dot(a, b, preferred_element_type=F32)


def one(mask):
    return jnp.where(mask, 1.0, 0.0).astype(BF)


def iota(shape, dim):
    return lax.broadcasted_iota(I32, shape, dim)


class Place:
    def __init__(self, planes, groups):
        self.planes, self.groups = planes, groups
        index = lax.axis_index("expert")
        self.z, self.k, self.x = index // PLANE, index % PLANE, lax.axis_index("dp")

    def mate(self, d):
        spot = lax.rem(self.k + d, PLANE)
        return spot, (self.z * PLANE + spot, self.x)

    def above(self, d):
        spot = lax.rem(self.z + d, self.planes)
        return spot, (spot * PLANE + self.k, self.x)

    def group(self, d):
        spot = lax.rem(self.x + d, self.groups)
        return spot, (self.z * PLANE + self.k, spot)

    def greet(self):
        barrier = pltpu.get_barrier_semaphore()
        peers = [self.mate(d)[1] for d in range(1, PLANE)]
        peers += [self.above(d)[1] for d in range(1, self.planes)]
        peers += [self.group(d)[1] for d in range(1, self.groups)]
        for peer in peers:
            pl.semaphore_signal(barrier, inc=1, device_id=peer, device_id_type=MESH)
        pl.semaphore_wait(barrier, len(peers))


def remote(src, dst, send, recv, peer):
    return pltpu.make_async_remote_copy(
        src_ref=src, dst_ref=dst, send_sem=send, recv_sem=recv, device_id=peer, device_id_type=MESH
    )


def far_first(i, count):
    half, sign = (i + 1) // 2, 2 * lax.rem(i, 2) - 1
    return lax.rem(count // 2 + sign * half, count)


def block(index, size):
    return pl.ds(pl.multiple_of(index * size, size), size)


def loop(low, high, step):
    def run(i, carry):
        step(i)
        return carry

    lax.fori_loop(low, high, run, 0)


def dispatch_kernel(
    planes, groups, cap,
    tok_ref, cot_ref, picks_ref,
    tin_ref, cin_ref, row_ref, rank_ref, flag_ref,
    picks_all, maps, flags, rows_pad, tall, pool, packed, hot, pick_hot, got, parts,
    pick_sem, map_sem, flag_sem, pool_sem, z_sem, part_sem, own_sem,
):
    me = Place(planes, groups)
    z, k, x = me.z, me.k, me.x
    tok, model = tok_ref.shape
    slots = picks_ref.shape[1]
    width = model // PLANE
    n_dev = planes * PLANE
    all_slots = PLANE * slots
    me.greet()

    def pick_copy(d):
        return remote(picks_ref, picks_all.at[k], pick_sem.at[0, d], pick_sem.at[1, d], me.mate(d)[1])

    def pool_copy(which, d):
        spot, peer = me.mate(d)
        return remote(
            (tok_ref, cot_ref)[which].at[:, block(spot, width)],
            pool.at[which, block(k, tok)],
            pool_sem.at[0, which, d], pool_sem.at[1, which, d], peer,
        )

    for d in range(1, PLANE):
        pick_copy(d).start()
    for which in range(2):
        for d in range(1, PLANE):
            pool_copy(which, d).start()
    own = [
        pltpu.make_async_copy(
            (tok_ref, cot_ref)[which].at[:, block(k, width)], pool.at[which, block(k, tok)], own_sem.at[which]
        )
        for which in range(2)
    ]
    for copy in own:
        copy.start()
    picks_all[k] = picks_ref[...]
    for d in range(1, PLANE):
        pick_copy(d).wait_recv()

    names = jnp.concatenate([picks_all[i] for i in range(PLANE)], axis=1)
    high, low = names // tok, lax.rem(names, tok)
    high_hot = iota((n_dev, all_slots), 0) == high
    low_hot = one(iota((tok, all_slots), 0) == low)
    tall[...] = low_hot
    count = lax.dot_general(
        one(high_hot), low_hot, (((1,), (1,)), ((), ())), preferred_element_type=F32
    )
    need = count > 0.5
    need_one = one(need)
    before = one(iota((tok, tok), 0) < iota((tok, tok), 1))
    row_a, row_b = iota((n_dev, n_dev), 0), iota((n_dev, n_dev), 1)
    earlier = one((row_b < row_a) & (row_b // PLANE == row_a // PLANE))
    rank = dot(need_one, before) + jnp.sum(dot(earlier, need_one), axis=1, keepdims=True)
    over = jnp.max(jnp.where(need & (rank > cap - 0.5), 1, 0), axis=(0, 1), keepdims=True)
    ranked = jnp.where(need, rank.astype(I32), -1)
    for p in range(planes):
        maps[p, 0:PLANE] = ranked[p * PLANE : (p + 1) * PLANE]
        maps[p, PLANE : 2 * PLANE] = jnp.broadcast_to(over, (PLANE, tok))

    def map_copy(d):
        spot, peer = me.above(d)
        return remote(maps.at[spot], rank_ref.at[z], map_sem.at[0, d], map_sem.at[1, d], peer)

    for d in range(1, planes):
        map_copy(d).start()
    rank_ref[z] = maps[z]

    rank_hi = jnp.floor(rank * (1.0 / 32.0))
    rank_lo = rank - 32.0 * rank_hi
    found = 32.0 * dot(rank_hi.astype(BF), tall[...]) + dot(rank_lo.astype(BF), tall[...])
    slot_rank = jnp.sum(jnp.where(high_hot, found, 0.0), axis=0, keepdims=True).astype(I32)
    slot_row = jnp.where(slot_rank < cap, (high // PLANE) * cap + slot_rank, -1)
    row_ref[...] = slot_row

    for d in range(1, planes):
        map_copy(d).wait_recv()
    over_group = jnp.max(rank_ref[:, PLANE : 2 * PLANE, :], axis=0)
    flags[x] = over_group

    def flag_copy(d):
        return remote(flags.at[x], flags.at[x], flag_sem.at[0, d], flag_sem.at[1, d], me.group(d)[1])

    for d in range(1, groups):
        flag_copy(d).start()

    def z_copy(which, d):
        return remote(
            packed.at[which, d], got.at[which, block(z, cap)],
            z_sem.at[0, which, d], z_sem.at[1, which, d], me.above(d)[1],
        )

    def fill_hot(d):
        spot = lax.rem(z + d, planes)
        rank_map = rank_ref[spot, 0:PLANE]
        for h in range(PLANE):
            hot[d, :, h * tok : (h + 1) * tok] = one(iota((cap, tok), 0) == rank_map[h : h + 1, :])

    def pack(which, d):
        return dot(hot[d], pool[which]).astype(BF)

    def send_tokens(i):
        d = far_first(i, planes)
        fill_hot(d)
        packed[0, d] = pack(0, d)
        z_copy(0, d).start()

    own[0].wait()
    for d in range(1, PLANE):
        pool_copy(0, d).wait_recv()
    loop(0, planes - 1, send_tokens)
    fill_hot(0)
    got[0, block(z, cap)] = pack(0, 0)

    def send_cots(i):
        d = far_first(i, planes)
        packed[1, d] = pack(1, d)
        z_copy(1, d).start()

    own[1].wait()
    for d in range(1, PLANE):
        pool_copy(1, d).wait_recv()
    loop(0, planes - 1, send_cots)
    got[1, block(z, cap)] = pack(1, 0)

    for b in range(all_slots // tok):
        rows_pad[b : b + 1, :] = slot_row[:, b * tok : (b + 1) * tok].astype(F32)
    turned = rows_pad[...].T.astype(I32)
    for b in range(all_slots // tok):
        pick_hot[b * tok : (b + 1) * tok, :] = one(
            iota((tok, planes * cap), 1) == turned[:, b : b + 1]
        )

    def part_copy(which, d):
        return remote(
            parts.at[which, d], (tin_ref, cin_ref)[which].at[:, block(k, width)],
            part_sem.at[0, which, d], part_sem.at[1, which, d], me.mate(d)[1],
        )

    for which in range(2):
        for d in range(1, planes):
            z_copy(which, d).wait_recv()

        def select(d, which=which):
            spot = lax.rem(k + d, PLANE)
            parts[which, d] = dot(pick_hot[block(spot, slots)], got[which]).astype(BF)

        def select_send(d, which=which):
            select(d)
            part_copy(which, d).start()

        loop(1, PLANE, select_send)
        select(0)
        home = pltpu.make_async_copy(
            parts.at[which, 0], (tin_ref, cin_ref)[which].at[:, block(k, width)], own_sem.at[which]
        )
        home.start()
        home.wait()

    for d in range(1, groups):
        flag_copy(d).wait()
    flag_ref[...] = jnp.max(flags[...], axis=0)
    for which in range(2):
        for d in range(1, PLANE):
            part_copy(which, d).wait()
            pool_copy(which, d).wait_send()
        for d in range(1, planes):
            z_copy(which, d).wait_send()
    for d in range(1, PLANE):
        pick_copy(d).wait_send()
    for d in range(1, planes):
        map_copy(d).wait_send()


def dispatch(planes, groups, cap, ident, tokens, cotangent, picks):
    tok, model = tokens.shape
    slots = picks.shape[1]
    width = model // PLANE
    all_slots = PLANE * slots
    dma = pltpu.SemaphoreType.DMA
    return pl.pallas_call(
        partial(dispatch_kernel, planes, groups, cap),
        out_shape=(
            jax.ShapeDtypeStruct((slots, model), BF),
            jax.ShapeDtypeStruct((slots, model), BF),
            jax.ShapeDtypeStruct((1, all_slots), I32),
            jax.ShapeDtypeStruct((planes, 2 * PLANE, tok), I32),
            jax.ShapeDtypeStruct((PLANE, tok), I32),
        ),
        in_specs=[VMEM] * 3,
        out_specs=[VMEM] * 5,
        scratch_shapes=[
            pltpu.VMEM((PLANE, 1, slots), I32),
            pltpu.VMEM((planes, 2 * PLANE, tok), I32),
            pltpu.VMEM((groups, PLANE, tok), I32),
            pltpu.VMEM((tok, tok), F32),
            pltpu.VMEM((tok, all_slots), BF),
            pltpu.VMEM((2, PLANE * tok, width), BF),
            pltpu.VMEM((2, planes, cap, width), BF),
            pltpu.VMEM((planes, cap, PLANE * tok), BF),
            pltpu.VMEM((all_slots, planes * cap), BF),
            pltpu.VMEM((2, planes * cap, width), BF),
            pltpu.VMEM((2, PLANE, slots, width), BF),
            dma((2, PLANE)),
            dma((2, planes)),
            dma((2, groups)),
            dma((2, 2, PLANE)),
            dma((2, 2, planes)),
            dma((2, 2, PLANE)),
            dma((2,)),
        ],
        compiler_params=pltpu.CompilerParams(
            collective_id=ident, has_side_effects=True, vmem_limit_bytes=60 * 2**20
        ),
        name=f"dispatch_{cap}",
    )(tokens, cotangent, picks)


def combine_kernel(
    planes, groups, cap,
    con_ref, dtk_ref, row_ref, rank_ref, tin_ref, dout_ref, hid_ref, dpre_ref,
    mixed_ref, gtok_ref, tins_ref, douts_ref, hids_ref, dpres_ref,
    msgs, row_hot, sums, got, ranks_pad, back_hot, final,
    msg_sem, z_sem, final_sem, x_sem, own_sem,
):
    me = Place(planes, groups)
    z, k, x = me.z, me.k, me.x
    slots, model = con_ref.shape
    tok = mixed_ref.shape[0]
    width = model // PLANE
    all_slots = PLANE * slots
    stride = got.shape[1] // planes
    part = model // groups
    me.greet()

    def msg_copy(which, d):
        spot, peer = me.mate(d)
        return remote(
            (con_ref, dtk_ref)[which].at[:, block(spot, width)], msgs.at[which, block(k, slots)],
            msg_sem.at[0, which, d], msg_sem.at[1, which, d], peer,
        )

    def x_copy(which, d):
        spot, peer = me.group(d)
        src = (
            hid_ref, dpre_ref, tin_ref.at[:, block(spot, part)], dout_ref.at[:, block(spot, part)]
        )[which]
        dst = (hids_ref, dpres_ref, tins_ref, douts_ref)[which].at[x]
        return remote(src, dst, x_sem.at[0, which, d], x_sem.at[1, which, d], peer)

    own = []
    for which in range(2):
        for d in range(1, PLANE):
            msg_copy(which, d).start()
        own.append(
            pltpu.make_async_copy(
                (con_ref, dtk_ref)[which].at[:, block(k, width)], msgs.at[which, block(k, slots)],
                own_sem.at[which],
            )
        )
    for which in range(4):
        for d in range(1, groups):
            x_copy(which, d).start()
        src = (hid_ref, dpre_ref, tin_ref.at[:, block(x, part)], dout_ref.at[:, block(x, part)])[which]
        dst = (hids_ref, dpres_ref, tins_ref, douts_ref)[which].at[x]
        own.append(pltpu.make_async_copy(src, dst, own_sem.at[2 + which]))
    for copy in own:
        copy.start()

    def z_copy(which, d):
        return remote(
            sums.at[which, d],
            got.at[which, pl.ds(pl.multiple_of(z * stride, stride), cap)],
            z_sem.at[0, which, d], z_sem.at[1, which, d], me.above(d)[1],
        )

    def fill(d):
        spot = lax.rem(z + d, planes)
        row_hot[d] = one(iota((cap, all_slots), 0) + spot * cap == row_ref[...])

    def add_up(which, d):
        return dot(row_hot[d], msgs[which]).astype(BF)

    for which in range(2):
        if which == 0:
            fill(0)
        own[which].wait()
        for d in range(1, PLANE):
            msg_copy(which, d).wait_recv()

        def send_sums(i, which=which):
            d = far_first(i, planes)
            if which == 0:
                fill(d)
            sums[which, d] = add_up(which, d)
            z_copy(which, d).start()

        loop(0, planes - 1, send_sums)
        got[which, pl.ds(pl.multiple_of(z * stride, stride), cap)] = add_up(which, 0)

    if stride > cap:
        for which in range(2):
            for p in range(planes):
                got[which, p * stride + cap : (p + 1) * stride] = jnp.zeros((stride - cap, width), BF)

    for p in range(planes):
        ranks_pad[p * PLANE : (p + 1) * PLANE] = rank_ref[p, 0:PLANE].astype(F32)
    turned = ranks_pad[...].T.astype(I32)
    for h in range(PLANE):
        for p in range(planes):
            c = p * PLANE + h
            back_hot[h * tok : (h + 1) * tok, p * stride : (p + 1) * stride] = one(
                iota((tok, stride), 1) == turned[:, c : c + 1]
            )

    def final_copy(which, d):
        return remote(
            final.at[which, d], (mixed_ref, gtok_ref)[which].at[:, block(k, width)],
            final_sem.at[0, which, d], final_sem.at[1, which, d], me.mate(d)[1],
        )

    for which in range(2):
        for d in range(1, planes):
            z_copy(which, d).wait_recv()

        def total(d, which=which):
            spot = lax.rem(k + d, PLANE)
            final[which, d] = dot(back_hot[block(spot, tok)], got[which]).astype(BF)

        def total_send(d, which=which):
            total(d)
            final_copy(which, d).start()

        loop(1, PLANE, total_send)
        total(0)
        home = pltpu.make_async_copy(
            final.at[which, 0], (mixed_ref, gtok_ref)[which].at[:, block(k, width)], own_sem.at[which]
        )
        home.start()
        home.wait()

    for which in range(2):
        for d in range(1, PLANE):
            final_copy(which, d).wait()
            msg_copy(which, d).wait_send()
        for d in range(1, planes):
            z_copy(which, d).wait_send()
    for which in range(4):
        own[2 + which].wait()
        for d in range(1, groups):
            x_copy(which, d).wait()


def combine(planes, groups, cap, ident, contrib, d_token, row, rank, token_in, d_out, hidden, d_pre):
    slots, model = contrib.shape
    tok = rank.shape[2]
    width = model // PLANE
    all_slots = PLANE * slots
    stride = -(-cap // 128) * 128
    dma = pltpu.SemaphoreType.DMA
    return pl.pallas_call(
        partial(combine_kernel, planes, groups, cap),
        out_shape=(
            jax.ShapeDtypeStruct((tok, model), BF),
            jax.ShapeDtypeStruct((tok, model), BF),
            jax.ShapeDtypeStruct((groups, slots, model // groups), BF),
            jax.ShapeDtypeStruct((groups, slots, model // groups), BF),
            jax.ShapeDtypeStruct((groups,) + hidden.shape, BF),
            jax.ShapeDtypeStruct((groups,) + d_pre.shape, BF),
        ),
        in_specs=[VMEM] * 8,
        out_specs=[VMEM] * 6,
        scratch_shapes=[
            pltpu.VMEM((2, all_slots, width), BF),
            pltpu.VMEM((planes, cap, all_slots), BF),
            pltpu.VMEM((2, planes, cap, width), BF),
            pltpu.VMEM((2, planes * stride, width), BF),
            pltpu.VMEM((tok, tok), F32),
            pltpu.VMEM((PLANE * tok, planes * stride), BF),
            pltpu.VMEM((2, PLANE, tok, width), BF),
            dma((2, 2, PLANE)),
            dma((2, 2, planes)),
            dma((2, 2, PLANE)),
            dma((2, 4, groups)),
            dma((6,)),
        ],
        compiler_params=pltpu.CompilerParams(
            collective_id=ident, has_side_effects=True, vmem_limit_bytes=60 * 2**20
        ),
        name=f"combine_{cap}",
    )(contrib, d_token, row, rank, token_in, d_out, hidden, d_pre)


def gelu_pair(pre_act):
    return jax.vjp(partial(jax.nn.gelu, approximate=True), pre_act)


def body(tokens, cotangent, picks, valid, comb, w_in, w_out):
    planes = lax.axis_size("expert") // PLANE
    groups = lax.axis_size("dp")
    loose = PLANE * min(tokens.shape[1], PLANE * MOST)
    names = picks[0]
    sent = dispatch(planes, groups, TIGHT, 0, tokens[0], cotangent[0], names)
    over = jnp.max(sent[4]) > 0
    token_in, cot_in, row, rank = lax.cond(
        over,
        lambda: tuple(dispatch(planes, groups, loose, 1, tokens[0], cotangent[0], names)[:4]),
        lambda: tuple(sent[:4]),
    )
    slot_scale = (comb[0, 0] * valid[0, 0].astype(F32))[:, None]
    pre_act = dot(token_in, w_in[0])
    act_value, act_back = gelu_pair(pre_act)
    hidden = act_value.astype(BF)
    contrib = (slot_scale * dot(hidden, w_out[0])).astype(BF)
    d_out = (slot_scale * cot_in.astype(F32)).astype(BF)
    d_hidden = lax.dot_general(d_out, w_out[0], (((1,), (1,)), ((), ())), preferred_element_type=F32)
    d_pre = act_back(d_hidden)[0].astype(BF)
    d_token = lax.dot_general(
        d_pre, w_in[0], (((1,), (1,)), ((), ())), preferred_element_type=F32
    ).astype(BF)
    operands = (contrib, d_token, row, rank, token_in, d_out, hidden, d_pre)
    mixed, grad_tokens, tins, douts, hids, dpres = lax.cond(
        over,
        lambda *a: tuple(combine(planes, groups, loose, 3, *a)),
        lambda *a: tuple(combine(planes, groups, TIGHT, 2, *a)),
        *operands,
    )
    over_rows = (((0, 1), (0, 1)), ((), ()))
    grad_in = lax.dot_general(tins, dpres, over_rows, preferred_element_type=F32).astype(BF)
    grad_out = lax.dot_general(hids, douts, over_rows, preferred_element_type=F32).astype(BF)
    return (mixed[None], grad_tokens[None], grad_in[None], grad_out[None])


def solution(mesh):
    placed = (
        P("dp", "expert", None),
        P("dp", "expert", None),
        P("dp", "expert", None),
        P("dp", "expert", None),
        P("dp", "expert", None),
        P("expert", None, None),
        P("expert", None, None),
    )
    return jax.shard_map(
        body,
        mesh=mesh,
        in_specs=placed,
        out_specs=(
            P("dp", "expert", None),
            P("dp", "expert", None),
            P("expert", "dp", None),
            P("expert", None, "dp"),
        ),
        check_vma=False,
    )
```

time: 311 us -> 202 us (0.65); the launches traced: 305 us -> 200 us
  Pallas kernels: 0 us -> 177 us
  waiting for transfers between devices: 124 us -> 0 us
  blocking collectives: 77.4 us -> 0 us
  other arithmetic: 24.9 us -> 2.25 us
  local copies, waits for them, and re-layouts: 24.2 us -> 2.54 us
  starting transfers between devices: 17.5 us -> 0 us
  between operations: 14.5 us -> 1.4 us
  matrix products: 22.6 us -> 16.5 us
    pallas_call x0 -> x2, Pallas kernels: none -> 177 us  [the longest x1 90.8 us: dispatch(): pl.pallas_call(partial(dispatch_kernel, planes, groups, cap), out_shape=(...]
    all_to_all x3 -> x0, waiting for transfers between devices: 124 us -> none  [the longest x1 45.8 us: body(): lax.all_to_all(pull(cotangent), 'expert', split_axis=0, concat_axis=0, ti...]
    all_to_all x2 -> x0, blocking collectives: 77.4 us -> none  [the longest x1 55.8 us: body(): lax.all_to_all(pull(tokens), 'expert', split_axis=0, concat_axis=0, tiled...]
    scatter-add x2 -> x0, other arithmetic: 16.7 us -> none  [spread(): total.at[asked_flat]]
    all_to_all x3 -> x0, starting transfers between devices: 16.6 us -> none  [the longest x1 5.77 us: body(): lax.all_to_all(place(contrib), 'expert', split_axis=0, concat_axis=0, til...]
    gather x4 -> x0, local copies, waits for them, and re-layouts: 13.3 us -> none  [the longest x2 7.52 us: compact(): jnp.take(received.reshape(-1, model_width), slot_flat, axis=0)]
    scatter x3 -> x0, local copies, waits for them, and re-layouts: 9.56 us -> none  [the longest x2 8.16 us: place(): return buffer.at[slot_flat].set(slot_rows.reshape(-1, model_width)).resha...]
    dot_general x6, matrix products: 22.6 us -> 16.5 us  [the longest x2 5.06 us: dot(): return jnp.dot(a, b, preferred_element_type=F32)]
  transfers between devices with their start and end apart: 5 -> 0, of which waited for: 3 -> 0; matrix products, arithmetic and copies ran while one was open for 15% -> 0% of each run, Pallas kernels for 0% -> 0%
where the time goes in v1:
time: 202 us; the launch traced here: 200 us
  Pallas kernels  177 us (88%)
  matrix products  16.5 us (8%)
  local copies, waits for them, and re-layouts  2.54 us (1%)
  other arithmetic  2.25 us (1%)
    pallas_call x1, Pallas kernels, dispatch(): pl.pallas_call(partial(dispatch_kernel, planes, groups, cap), out_shape=(...  90.8 us
    pallas_call x1, Pallas kernels, combine(): pl.pallas_call(partial(combine_kernel, planes, groups, cap), out_shape=(j...  86.1 us
    dot_general x2, matrix products, dot(): return jnp.dot(a, b, preferred_element_type=F32)  5.06 us
    dot_general x1, matrix products, body(): lax.dot_general(tins, dpres, over_rows, preferred_element_type=F32)  4.3 us

profile of v1, /device:TPU:6, one launch (start us, length us, event | category | flops | bytes accessed | tf_op | source)
XLA Modules:
  0.0 200.3 jit_solution(1587465769220567066)
XLA Ops:
  0.6 0.7 convert_multiply_fusion.1
  1.3 90.8 %dispatch_304.1 = (bf16[256,2048]{1,0:T(8,128)(2,1)S(1)}, bf16[256,2048]{1,0:T(8,128)(2,1)S(1)}, s32[1,2048]{1,0:T(1,128)S(1)}, s32[8,16,128]{2,1,0:T(8,128)S(1)}, s32[8,128]{1,0:T(8,128)}) custom-call(bf16[128,2048]{1,0:T(8,128)(2,1)} %bitcast.50, bf16[128,2048]{1,0:T(8,128)(2,1)} %bitcast.52, s32[1,256]{1,0:T(1,128)} %bitcast.58), custom_call_target="tpu_custom_call" | custom-call | tf_op jit(solution)/shard_map/dispatch_304/pallas_call | solution.py:267
  92.2 1.3 reduce_max.9
  94.1 0.4 conditional.2
  94.6 0.0 copy-start
  94.6 0.2 fusion.17
  94.8 0.0 copy-start.3
  94.8 3.8 %multiply_convert_fusion = (bf16[256,1024]{1,0:T(8,128)(2,1)S(1)}, f32[256,1024]{1,0:T(8,128)S(1)}) fusion(bf16[256,2048]{1,0:T(8,128)(2,1)S(1)} %get-tuple-element.152, bf16[1,2048,1024]{2,1,0:T(8,128)(2,1)} %param.16), kind=kOutput, calls=%fused_computation.26 | convolution fusion | flops 1076101120 | bytes 6815744 | tf_op jit(solution)/shard_map/dot_general | solution.py:21
  98.6 0.0 copy-done
  98.6 0.0 copy-done.3
  98.7 2.6 %fusion.26 = bf16[256,1024]{1,0:T(8,128)(2,1)} fusion(f32[256,1024]{1,0:T(8,128)S(1)} %get-tuple-element.157, bf16[256,2048]{1,0:T(8,128)(2,1)S(1)} %fusion.17, bf16[1,1024,2048]{2,1,0:T(8,128)(2,1)S(1)} %copy-done.3), kind=kOutput, calls=%fused_computation.25 | convolution fusion | flops 1078984704 | bytes 6815744 | tf_op jit(solution)/shard_map/dot_general | solution.py:502
  101.2 0.0 copy-start.4
  101.2 1.3 fusion.11
  102.5 0.9 copy-done.4
  103.4 2.3 %fusion.14 = bf16[256,2048]{1,0:T(8,128)(2,1)S(1)} fusion(bf16[256,1024]{1,0:T(8,128)(2,1)} %fusion.26, bf16[1,2048,1024]{2,1,0:T(8,128)(2,1)S(1)} %copy-done.4), kind=kOutput, calls=%fused_computation.10 | convolution fusion | flops 1074266112 | bytes 5767168 | tf_op jit(solution)/shard_map/dot_general | solution.py:504
  105.7 86.3 %conditional.3 = (bf16[4,256,512]{2,1,0:T(8,128)(2,1)}, bf16[4,256,512]{2,1,0:T(8,128)(2,1)}, bf16[4,256,1024]{2,1,0:T(8,128)(2,1)}, bf16[4,256,1024]{2,1,0:T(8,...) conditional(s32[]{:T(128)} %convert_element_type.39, (bf16[256,2048]{1,0:T(8,128)(2,1)S(1)}, ...), branch_computations={%region_3.0_spmd, %region_4.0_spmd} | conditional | bytes 48 | solution.py:508
  105.8 86.1 %combine_304.1 = (bf16[128,2048]{1,0:T(8,128)(2,1)}, bf16[128,2048]{1,0:T(8,128)(2,1)}, bf16[4,256,512]{2,1,0:T(8,128)(2,1)}, bf16[4,256,512]{2,1,0:T(8,128)(2,1...) custom-call(bf16[256,2048]{1,0:T(8,128)(2,1)S(1)} %get-tuple-element.83.con_ref, ...), custom_call_target="tpu_custom_call" | custom-call | tf_op jit(solution)/shard_map/cond/branch_0_fun/combine_304/pallas_call | solution.py:447
  192.1 0.0 copy-start.5
  192.1 0.0 copy-start.6
  192.1 4.3 %fusion.18 = bf16[1,512,1024]{2,1,0:T(8,128)(2,1)} fusion(bf16[4,256,512]{2,1,0:T(8,128)(2,1)} %get-tuple-element.129, bf16[4,256,1024]{2,1,0:T(8,128)(2,1)} %get-tuple-element.130), kind=kOutput, calls=%fused_computation.17 | convolution fusion | flops 1074266112 | bytes 4194304 | tf_op jit(solution)/shard_map/dot_general | solution.py:515
  196.4 0.0 copy-done.5
  196.4 0.0 copy-done.6
  196.4 0.0 copy-start.1
  196.4 0.0 copy-start.2
  196.4 2.3 %fusion.19 = bf16[1,1024,512]{2,1,0:T(8,128)(2,1)} fusion(bf16[4,256,1024]{2,1,0:T(8,128)(2,1)S(1)} %copy-done.5, bf16[4,256,512]{2,1,0:T(8,128)(2,1)S(1)} %copy-done.6), kind=kOutput, calls=%fused_computation.18 | convolution fusion | flops 1074266112 | bytes 4194304 | tf_op jit(solution)/shard_map/dot_general | solution.py:516
  198.7 0.0 copy-done.1
  198.7 0.8 copy.37
  199.5 0.0 copy-done.2
  199.5 0.8 copy.38
Async XLA Ops:
  94.6 4.1 %copy-start = (bf16[256,2048]{1,0:T(8,128)(2,1)}, bf16[256,2048]{1,0:T(8,128)(2,1)S(1)}, u32[]{:S(2)}) copy-start(bf16[256,2048]{1,0:T(8,128)(2,1)S(1)} %get-tuple-element.152) | copy-start | bytes 3145732
  94.8 3.8 %copy-start.3 = (bf16[1,1024,2048]{2,1,0:T(8,128)(2,1)S(1)}, bf16[1,1024,2048]{2,1,0:T(8,128)(2,1)}, u32[]{:S(2)}) copy-start(bf16[1,1024,2048]{2,1,0:T(8,128)(2,1)} %param.17) | copy-start | bytes 12582916
  101.2 2.2 %copy-start.4 = (bf16[1,2048,1024]{2,1,0:T(8,128)(2,1)S(1)}, bf16[1,2048,1024]{2,1,0:T(8,128)(2,1)}, u32[]{:S(2)}) copy-start(bf16[1,2048,1024]{2,1,0:T(8,128)(2,1)} %param.16) | copy-start | bytes 12582916
  192.1 4.3 %copy-start.5 = (bf16[4,256,1024]{2,1,0:T(8,128)(2,1)S(1)}, bf16[4,256,1024]{2,1,0:T(8,128)(2,1)}, u32[]{:S(2)}) copy-start(bf16[4,256,1024]{2,1,0:T(8,128)(2,1)} %get-tuple-element.131) | copy-start | bytes 6291460
  192.1 4.3 %copy-start.6 = (bf16[4,256,512]{2,1,0:T(8,128)(2,1)S(1)}, bf16[4,256,512]{2,1,0:T(8,128)(2,1)}, u32[]{:S(2)}) copy-start(bf16[4,256,512]{2,1,0:T(8,128)(2,1)} %get-tuple-element.132) | copy-start | bytes 3145732
  196.4 2.3 %copy-start.1 = (bf16[1,128,2048]{2,1,0:T(8,128)(2,1)S(1)}, bf16[1,128,2048]{2,1,0:T(8,128)(2,1)}, u32[]{:S(2)}) copy-start(bf16[1,128,2048]{2,1,0:T(8,128)(2,1)} %get-tuple-element.182) | copy-start | bytes 1572868
  196.4 3.1 %copy-start.2 = (bf16[1,128,2048]{2,1,0:T(8,128)(2,1)S(1)}, bf16[1,128,2048]{2,1,0:T(8,128)(2,1)}, u32[]{:S(2)}) copy-start(bf16[1,128,2048]{2,1,0:T(8,128)(2,1)} %get-tuple-element.183) | copy-start | bytes 1572868

commit v2 on v0

v2 whole, which is shorter than its diff:
```python
from functools import partial

import jax
import jax.numpy as jnp
from jax import lax
from jax.experimental import pallas as pl
from jax.experimental.pallas import tpu as pltpu
from jax.sharding import PartitionSpec as P

MESH = pl.DeviceIdType.MESH
PLANE = 8
MOST = 8
LIMIT = 63
TIGHT = 304
VMEM = pl.BlockSpec(memory_space=pltpu.VMEM)
BF = jnp.bfloat16
F32 = jnp.float32
I32 = jnp.int32


def dot(a, b):
    return jnp.dot(a, b, preferred_element_type=F32)


def one(mask):
    return jnp.where(mask, 1.0, 0.0).astype(BF)


def iota(shape, dim):
    return lax.broadcasted_iota(I32, shape, dim)


class Place:
    def __init__(self, planes, groups):
        self.planes, self.groups = planes, groups
        index = lax.axis_index("expert")
        self.z, self.k, self.x = index // PLANE, index % PLANE, lax.axis_index("dp")

    def mate(self, d):
        spot = lax.rem(self.k + d, PLANE)
        return spot, (self.z * PLANE + spot, self.x)

    def above(self, d):
        spot = lax.rem(self.z + d, self.planes)
        return spot, (spot * PLANE + self.k, self.x)

    def group(self, d):
        spot = lax.rem(self.x + d, self.groups)
        return spot, (self.z * PLANE + self.k, spot)

    def greet(self):
        barrier = pltpu.get_barrier_semaphore()
        peers = [self.mate(d)[1] for d in range(1, PLANE)]
        peers += [self.above(d)[1] for d in range(1, self.planes)]
        peers += [self.group(d)[1] for d in range(1, self.groups)]
        for peer in peers:
            pl.semaphore_signal(barrier, inc=1, device_id=peer, device_id_type=MESH)
        pl.semaphore_wait(barrier, len(peers))


def remote(src, dst, send, recv, peer):
    return pltpu.make_async_remote_copy(
        src_ref=src, dst_ref=dst, send_sem=send, recv_sem=recv, device_id=peer, device_id_type=MESH
    )


def far_first(i, count):
    half, sign = (i + 1) // 2, 2 * lax.rem(i, 2) - 1
    return lax.rem(count // 2 + sign * half, count)


def block(index, size):
    return pl.ds(pl.multiple_of(index * size, size), size)


def dot_nt(a, b):
    return lax.dot_general(a, b, (((1,), (1,)), ((), ())), preferred_element_type=F32)


def dot_tn(a, b):
    return lax.dot_general(a, b, (((0,), (0,)), ((), ())), preferred_element_type=F32)


def loop(low, high, step):
    def run(i, carry):
        step(i)
        return carry

    lax.fori_loop(low, high, run, 0)


def layer_kernel(
    planes, groups, cap, stored,
    tok_ref, cot_ref, picks_ref, scale_ref, w_in_ref, w_out_ref,
    mixed_ref, gtok_ref, gin_ref, gout_ref, flag_ref,
    picks_all, maps, ranks, flags, turn, slot_cols, back_cols, tall, pool, hot, packed, pick_hot, got,
    parts, taken, wi, wo, pre, slope, hid, d_pre, msgs, row_hot, home, back_hot, final,
    tins, douts, hids, dpres, rows,
    pick_sem, map_sem, flag_sem, pool_sem, z_sem, part_sem, msg_sem, back_sem, final_sem, x_sem, own_sem,
):
    me = Place(planes, groups)
    z, k, x = me.z, me.k, me.x
    tok, model = tok_ref.shape
    slots = picks_ref.shape[1]
    width = model // PLANE
    n_dev = planes * PLANE
    all_slots = PLANE * slots
    stride = home.shape[1] // planes
    per_group = PLANE // groups
    ffw = hid.shape[1]
    me.greet()

    def pick_copy(d):
        return remote(picks_ref, picks_all.at[k], pick_sem.at[0, d], pick_sem.at[1, d], me.mate(d)[1])

    def pool_copy(which, d):
        spot, peer = me.mate(d)
        return remote(
            (tok_ref, cot_ref)[which].at[:, block(spot, width)],
            pool.at[which, block(k, tok)],
            pool_sem.at[0, which, d], pool_sem.at[1, which, d], peer,
        )

    def map_copy(d):
        spot, peer = me.above(d)
        return remote(maps.at[spot], ranks.at[z], map_sem.at[0, d], map_sem.at[1, d], peer)

    def flag_copy(d):
        return remote(flags.at[x], flags.at[x], flag_sem.at[0, d], flag_sem.at[1, d], me.group(d)[1])

    def z_copy(which, d):
        return remote(
            packed.at[which, d], got.at[which, block(z, cap)],
            z_sem.at[0, which, d], z_sem.at[1, which, d], me.above(d)[1],
        )

    def part_copy(which, d):
        return remote(
            parts.at[which, d], taken.at[which, k],
            part_sem.at[0, which, d], part_sem.at[1, which, d], me.mate(d)[1],
        )

    def msg_copy(which, d):
        return remote(
            parts.at[which, d], msgs.at[which, block(k, slots)],
            msg_sem.at[0, which, d], msg_sem.at[1, which, d], me.mate(d)[1],
        )

    def back_copy(which, d):
        return remote(
            packed.at[which, d],
            home.at[which, pl.ds(pl.multiple_of(z * stride, stride), cap)],
            back_sem.at[0, which, d], back_sem.at[1, which, d], me.above(d)[1],
        )

    def final_copy(which, d):
        return remote(
            final.at[which, d], (mixed_ref, gtok_ref)[which].at[:, block(k, width)],
            final_sem.at[0, which, d], final_sem.at[1, which, d], me.mate(d)[1],
        )

    def x_pair(which, spot):
        src = (
            hid, d_pre, taken.at[0, pl.ds(spot * per_group, per_group)],
            taken.at[1, pl.ds(spot * per_group, per_group)],
        )[which]
        return src, (hids, dpres, tins, douts)[which].at[x]

    def x_copy(which, d):
        spot, peer = me.group(d)
        src, dst = x_pair(which, spot)
        return remote(src, dst, x_sem.at[0, which, d], x_sem.at[1, which, d], peer)

    def x_own(which):
        src, dst = x_pair(which, x)
        return pltpu.make_async_copy(src, dst, own_sem.at[2 + which])

    def x_start(which):
        for d in range(1, groups):
            x_copy(which, d).start()
        x_own(which).start()

    for d in range(1, PLANE):
        pick_copy(d).start()
    for which in range(2):
        for d in range(1, PLANE):
            pool_copy(which, d).start()
    own = [
        pltpu.make_async_copy(
            (tok_ref, cot_ref)[which].at[:, block(k, width)], pool.at[which, block(k, tok)], own_sem.at[which]
        )
        for which in range(2)
    ]
    weights = [
        pltpu.make_async_copy(w_in_ref, wi, own_sem.at[6]),
        pltpu.make_async_copy(w_out_ref, wo, own_sem.at[7]),
    ]
    for copy in own + weights:
        copy.start()
    picks_all[k] = picks_ref[...]
    if stride > cap:
        for which in range(2):
            for p in range(planes):
                home[which, p * stride + cap : (p + 1) * stride] = jnp.zeros((stride - cap, width), BF)
    for d in range(1, PLANE):
        pick_copy(d).wait_recv()

    names = jnp.concatenate([picks_all[i] for i in range(PLANE)], axis=1)
    high, low = names // tok, lax.rem(names, tok)
    high_hot = iota((n_dev, all_slots), 0) == high
    low_hot = one(iota((tok, all_slots), 0) == low)
    tall[...] = low_hot
    need = dot_nt(one(high_hot), low_hot) > 0.5
    need_one = one(need)
    before = one(iota((tok, tok), 0) < iota((tok, tok), 1))
    row_a, row_b = iota((n_dev, n_dev), 0), iota((n_dev, n_dev), 1)
    earlier = one((row_b < row_a) & (row_b // PLANE == row_a // PLANE))
    rank = dot(need_one, before) + jnp.sum(dot(earlier, need_one), axis=1, keepdims=True)
    over = jnp.max(jnp.where(need & (rank > cap - 0.5), 1, 0), axis=(0, 1), keepdims=True)
    ranked = jnp.where(need, rank.astype(I32), -1)
    for p in range(planes):
        maps[p, 0:PLANE] = ranked[p * PLANE : (p + 1) * PLANE]
        maps[p, PLANE : 2 * PLANE] = jnp.broadcast_to(over, (PLANE, tok))
    for d in range(1, planes):
        map_copy(d).start()
    ranks[z] = maps[z]

    rank_hi = jnp.floor(rank * (1.0 / 32.0))
    rank_lo = rank - 32.0 * rank_hi
    found = 32.0 * dot(rank_hi.astype(BF), tall[...]) + dot(rank_lo.astype(BF), tall[...])
    slot_rank = jnp.sum(jnp.where(high_hot, found, 0.0), axis=0, keepdims=True).astype(I32)
    rows[...] = jnp.where(slot_rank < cap, (high // PLANE) * cap + slot_rank, -1)

    for d in range(1, planes):
        map_copy(d).wait_recv()
    flags[x] = jnp.max(ranks[:, PLANE : 2 * PLANE, :], axis=0)
    for d in range(1, groups):
        flag_copy(d).start()

    def pack(which, d, slot):
        rank_map = ranks[lax.rem(z + d, planes), 0:PLANE]
        for h in range(PLANE):
            hot[slot, :, h * tok : (h + 1) * tok] = one(iota((cap, tok), 0) == rank_map[h : h + 1, :])
        return dot(hot[slot], pool[which]).astype(BF)

    for which in range(2):
        own[which].wait()
        for d in range(1, PLANE):
            pool_copy(which, d).wait_recv()

        def send_rows(i, which=which):
            d = far_first(i, planes)
            packed[which, d] = pack(which, d, 0)
            z_copy(which, d).start()

        loop(0, planes - 1, send_rows)
        got[which, block(z, cap)] = pack(which, 0, 1)

    for b in range(all_slots // tok):
        turn[b : b + 1, :] = rows[:, b * tok : (b + 1) * tok].astype(F32)
    turned = turn[...].T.astype(I32)
    per = slots // tok
    for b in range(all_slots // tok):
        slot_cols[b // per, (b % per) * tok : (b % per + 1) * tok] = jnp.broadcast_to(
            turned[:, b : b + 1], (tok, tok)
        )

    def fill_pick(spot, slot):
        pick_hot[slot] = one(iota((slots, planes * cap), 1) == slot_cols[spot][:, 0:1])

    if stored:
        loop(0, PLANE, lambda spot: fill_pick(spot, spot))

    def select_all(which):
        for d in range(1, planes):
            z_copy(which, d).wait_recv()

        def select(d):
            spot = lax.rem(k + d, PLANE)
            if not stored:
                fill_pick(spot, 0)
            return dot(pick_hot[spot if stored else 0], got[which]).astype(BF)

        def send(d):
            parts[which, d] = select(d)
            part_copy(which, d).start()

        loop(1, PLANE, send)
        taken[which, k] = select(0)

    def each_chunk(which, step):
        step(k, True)
        for d in range(1, PLANE):
            part_copy(which, d).wait_recv()
            step(lax.rem(k + PLANE - d, PLANE), False)

    select_all(0)
    for copy in weights:
        copy.wait()

    def project(c, first):
        term = dot(taken[0, c], wi[block(c, width)])
        pre[...] = term if first else pre[...] + term

    each_chunk(0, project)
    x_start(2)
    tile = 32

    def activate(i):
        v = pre[block(i, tile)]
        inner = 0.7978845608028654 * (v + 0.044715 * (v * v * v))
        t = jnp.tanh(inner)
        hid[block(i, tile)] = (0.5 * v * (1.0 + t)).astype(BF)
        bend = 0.7978845608028654 * (1.0 + 0.134145 * (v * v))
        slope[block(i, tile)] = 0.5 * (1.0 + t) + 0.5 * v * ((1.0 - t * t) * bend)

    loop(0, slots // tile, activate)
    x_start(0)
    scale = scale_ref[:, 0:1]

    def contribution(d):
        spot = lax.rem(k + d, PLANE)
        return (scale * dot(hid[...], wo[:, block(spot, width)])).astype(BF)

    def send_contribution(d):
        part_copy(0, d).wait_send()
        parts[0, d] = contribution(d)
        msg_copy(0, d).start()

    loop(1, PLANE, send_contribution)
    msgs[0, block(k, slots)] = contribution(0)

    select_all(1)

    def send_sums(which):
        for d in range(1, PLANE):
            msg_copy(which, d).wait_recv()

        def add_up(d, slot):
            spot = lax.rem(z + d, planes)
            row_hot[slot] = one(iota((cap, all_slots), 0) + spot * cap == rows[...])
            return dot(row_hot[slot], msgs[which]).astype(BF)

        def send(i):
            d = far_first(i, planes)
            z_copy(which, d).wait_send()
            packed[which, d] = add_up(d, 0)
            back_copy(which, d).start()

        loop(0, planes - 1, send)
        home[which, pl.ds(pl.multiple_of(z * stride, stride), cap)] = add_up(0, 1)

    send_sums(0)

    def pull_back(c, first):
        d_out = (scale * taken[1, c].astype(F32)).astype(BF)
        taken[1, c] = d_out
        term = dot_nt(d_out, wo[:, block(c, width)])
        pre[...] = term if first else pre[...] + term

    each_chunk(1, pull_back)

    def chain(i):
        d_pre[block(i, tile)] = (pre[block(i, tile)] * slope[block(i, tile)]).astype(BF)

    loop(0, slots // tile, chain)

    def token_grad(d):
        spot = lax.rem(k + d, PLANE)
        return dot_nt(d_pre[...], wi[block(spot, width)]).astype(BF)

    def send_token_grad(d):
        part_copy(1, d).wait_send()
        parts[1, d] = token_grad(d)
        msg_copy(1, d).start()

    loop(1, PLANE, send_token_grad)
    msgs[1, block(k, slots)] = token_grad(0)
    x_start(1)
    x_start(3)
    send_sums(1)

    for p in range(planes):
        for h in range(PLANE):
            turn[h * planes + p : h * planes + p + 1] = ranks[p, h : h + 1].astype(F32)
    turned_back = turn[...].T.astype(I32)
    for h in range(PLANE):
        back_cols[h, :, 0:planes] = turned_back[:, h * planes : (h + 1) * planes]

    def fill_back(spot, slot):
        cols = back_cols[spot]
        for p in range(planes):
            back_hot[slot, :, p * stride : (p + 1) * stride] = one(
                iota((tok, stride), 1) == cols[:, p : p + 1]
            )

    if stored:
        loop(0, PLANE, lambda spot: fill_back(spot, spot))

    def send_totals(which):
        for d in range(1, planes):
            back_copy(which, d).wait_recv()

        def total(d):
            spot = lax.rem(k + d, PLANE)
            if not stored:
                fill_back(spot, 0)
            final[which, d] = dot(back_hot[spot if stored else 0], home[which]).astype(BF)

        def send(d):
            total(d)
            final_copy(which, d).start()

        loop(1, PLANE, send)
        total(0)
        pltpu.make_async_copy(
            final.at[which, 0], (mixed_ref, gtok_ref)[which].at[:, block(k, width)], own_sem.at[which]
        ).start()

    send_totals(0)
    send_totals(1)

    for which in range(4):
        x_own(which).wait()
        for d in range(1, groups):
            x_copy(which, d).wait_recv()
    for h in range(per_group):
        total_in = dot_tn(tins[0, h], dpres[0])
        for g in range(1, groups):
            total_in += dot_tn(tins[g, h], dpres[g])
        gin_ref[h * width : (h + 1) * width] = total_in.astype(BF)

    def out_grad(m):
        for h in range(per_group):
            total_out = dot_tn(hids[0, :, block(m, width)], douts[0, h])
            for g in range(1, groups):
                total_out += dot_tn(hids[g, :, block(m, width)], douts[g, h])
            gout_ref[block(m, width), h * width : (h + 1) * width] = total_out.astype(BF)

    loop(0, ffw // width, out_grad)

    for d in range(1, groups):
        flag_copy(d).wait()
        for which in range(4):
            x_copy(which, d).wait_send()
    flag_ref[...] = jnp.max(flags[...], axis=0)
    for which in range(2):
        pltpu.make_async_copy(
            final.at[which, 0], (mixed_ref, gtok_ref)[which].at[:, block(k, width)], own_sem.at[which]
        ).wait()
        for d in range(1, PLANE):
            final_copy(which, d).wait()
            msg_copy(which, d).wait_send()
            pool_copy(which, d).wait_send()
        for d in range(1, planes):
            back_copy(which, d).wait_send()
    for d in range(1, PLANE):
        pick_copy(d).wait_send()
    for d in range(1, planes):
        map_copy(d).wait_send()


def layer(planes, groups, cap, stored, ident, tokens, cotangent, picks, scale, w_in, w_out):
    tok, model = tokens.shape
    slots = picks.shape[1]
    ffw = w_in.shape[1]
    width = model // PLANE
    all_slots = PLANE * slots
    stride = -(-cap // 128) * 128
    per_group = PLANE // groups
    keep = PLANE if stored else 1
    dma = pltpu.SemaphoreType.DMA
    return pl.pallas_call(
        partial(layer_kernel, planes, groups, cap, stored),
        out_shape=(
            jax.ShapeDtypeStruct((tok, model), BF),
            jax.ShapeDtypeStruct((tok, model), BF),
            jax.ShapeDtypeStruct((model // groups, ffw), BF),
            jax.ShapeDtypeStruct((ffw, model // groups), BF),
            jax.ShapeDtypeStruct((PLANE, tok), I32),
        ),
        in_specs=[VMEM] * 4 + [pl.BlockSpec(memory_space=pl.ANY)] * 2,
        out_specs=[VMEM] * 5,
        scratch_shapes=[
            pltpu.VMEM((PLANE, 1, slots), I32),
            pltpu.VMEM((planes, 2 * PLANE, tok), I32),
            pltpu.VMEM((planes, 2 * PLANE, tok), I32),
            pltpu.VMEM((groups, PLANE, tok), I32),
            pltpu.VMEM((tok, tok), F32),
            pltpu.VMEM((PLANE, slots, tok), I32),
            pltpu.VMEM((PLANE, tok, tok), I32),
            pltpu.VMEM((tok, all_slots), BF),
            pltpu.VMEM((2, PLANE * tok, width), BF),
            pltpu.VMEM((2, cap, PLANE * tok), BF),
            pltpu.VMEM((2, planes, cap, width), BF),
            pltpu.VMEM((keep, slots, planes * cap), BF),
            pltpu.VMEM((2, planes * cap, width), BF),
            pltpu.VMEM((2, PLANE, slots, width), BF),
            pltpu.VMEM((2, PLANE, slots, width), BF),
            pltpu.VMEM(w_in.shape, BF),
            pltpu.VMEM(w_out.shape, BF),
            pltpu.VMEM((slots, ffw), F32),
            pltpu.VMEM((slots, ffw), F32),
            pltpu.VMEM((slots, ffw), BF),
            pltpu.VMEM((slots, ffw), BF),
            pltpu.VMEM((2, all_slots, width), BF),
            pltpu.VMEM((2, cap, all_slots), BF),
            pltpu.VMEM((2, planes * stride, width), BF),
            pltpu.VMEM((keep, tok, planes * stride), BF),
            pltpu.VMEM((2, PLANE, tok, width), BF),
            pltpu.VMEM((groups, per_group, slots, width), BF),
            pltpu.VMEM((groups, per_group, slots, width), BF),
            pltpu.VMEM((groups, slots, ffw), BF),
            pltpu.VMEM((groups, slots, ffw), BF),
            pltpu.VMEM((1, all_slots), I32),
            dma((2, PLANE)),
            dma((2, planes)),
            dma((2, groups)),
            dma((2, 2, PLANE)),
            dma((2, 2, planes)),
            dma((2, 2, PLANE)),
            dma((2, 2, PLANE)),
            dma((2, 2, planes)),
            dma((2, 2, PLANE)),
            dma((2, 4, groups)),
            dma((8,)),
        ],
        compiler_params=pltpu.CompilerParams(
            collective_id=ident, has_side_effects=True, vmem_limit_bytes=LIMIT * 2**20
        ),
        name=f"layer_{cap}",
    )(tokens, cotangent, picks, scale, w_in, w_out)


def body(tokens, cotangent, picks, valid, comb, w_in, w_out):
    planes = lax.axis_size("expert") // PLANE
    groups = lax.axis_size("dp")
    loose = PLANE * min(tokens.shape[1], PLANE * MOST)
    scale = comb[0, 0] * valid[0, 0].astype(F32)
    scale = jnp.broadcast_to(scale[:, None], (scale.shape[0], 128))
    operands = (tokens[0], cotangent[0], picks[0], scale, w_in[0], w_out[0])
    results = layer(planes, groups, TIGHT, True, 0, *operands)
    results = lax.cond(
        jnp.max(results[4]) > 0,
        lambda: tuple(layer(planes, groups, loose, False, 1, *operands)[:4]),
        lambda: tuple(results[:4]),
    )
    return tuple(result[None] for result in results)


def solution(mesh):
    placed = (
        P("dp", "expert", None),
        P("dp", "expert", None),
        P("dp", "expert", None),
        P("dp", "expert", None),
        P("dp", "expert", None),
        P("expert", None, None),
        P("expert", None, None),
    )
    return jax.shard_map(
        body,
        mesh=mesh,
        in_specs=placed,
        out_specs=(
            P("dp", "expert", None),
            P("dp", "expert", None),
            P("expert", "dp", None),
            P("expert", None, "dp"),
        ),
        check_vma=False,
    )
```

time: 311 us -> 162 us (0.52); the launches traced: 305 us -> 161 us
  Pallas kernels: 0 us -> 150 us
  waiting for transfers between devices: 124 us -> 0 us
  blocking collectives: 77.4 us -> 0 us
  other arithmetic: 24.9 us -> 2.02 us
  matrix products: 22.6 us -> 0 us
  starting transfers between devices: 17.5 us -> 0 us
  local copies, waits for them, and re-layouts: 24.2 us -> 7.19 us
  between operations: 14.5 us -> 1.35 us
    pallas_call x0 -> x1, Pallas kernels: none -> 150 us  [layer(): pl.pallas_call(partial(layer_kernel, planes, groups, cap, stored), out_sh...]
    all_to_all x3 -> x0, waiting for transfers between devices: 124 us -> none  [the longest x1 45.8 us: body(): lax.all_to_all(pull(cotangent), 'expert', split_axis=0, concat_axis=0, ti...]
    all_to_all x2 -> x0, blocking collectives: 77.4 us -> none  [the longest x1 55.8 us: body(): lax.all_to_all(pull(tokens), 'expert', split_axis=0, concat_axis=0, tiled...]
    dot_general x6 -> x0, matrix products: 22.6 us -> none  [the longest x1 5.14 us: body(): jnp.einsum('kcf,kcd->kfd', hidden, d_out, preferred_element_type=jnp.floa...]
    scatter-add x2 -> x0, other arithmetic: 16.7 us -> none  [spread(): total.at[asked_flat]]
    all_to_all x3 -> x0, starting transfers between devices: 16.6 us -> none  [the longest x1 5.77 us: body(): lax.all_to_all(place(contrib), 'expert', split_axis=0, concat_axis=0, til...]
    gather x4 -> x0, local copies, waits for them, and re-layouts: 13.3 us -> none  [the longest x2 7.52 us: compact(): jnp.take(received.reshape(-1, model_width), slot_flat, axis=0)]
    scatter x3 -> x0, local copies, waits for them, and re-layouts: 9.56 us -> none  [the longest x2 8.16 us: place(): return buffer.at[slot_flat].set(slot_rows.reshape(-1, model_width)).resha...]
  transfers between devices with their start and end apart: 5 -> 0, of which waited for: 3 -> 0; matrix products, arithmetic and copies ran while one was open for 15% -> 0% of each run, Pallas kernels for 0% -> 0%
where the time goes in v2:
time: 162 us; the launch traced here: 161 us
  Pallas kernels  150 us (93%)
  local copies, waits for them, and re-layouts  7.19 us (4%)
  other arithmetic  2.02 us (1%)
    pallas_call x1, Pallas kernels, layer(): pl.pallas_call(partial(layer_kernel, planes, groups, cap, stored), out_sh...  150 us
    unnamed x10, local copies, waits for them, and re-layouts  7.1 us

profile of v2, /device:TPU:6, one launch (start us, length us, event | category | flops | bytes accessed | tf_op | source)
XLA Modules:
  0.0 160.8 jit_solution(7534393941188751991)
XLA Ops:
  0.6 0.7 convert_multiply_fusion
  1.3 0.1 broadcast_in_dim.34.scale_ref
  1.4 0.0 copy-start
  1.4 0.0 copy-start.2
  1.5 150.0 %layer_304.1 = (bf16[128,2048]{1,0:T(8,128)(2,1)}, bf16[128,2048]{1,0:T(8,128)(2,1)}, bf16[512,1024]{1,0:T(8,128)(2,1)}, bf16[1024,512]{1,0:T(8,128)(2,1)}, s32[8,128]{1,0:T(8,128)}) custom-call(bf16[128,2048]{1,0:T(8,128)(2,1)} %bitcast.18, bf16[128,2048]{1,0:T(8,128)(2,1)} %bitcast.20, s32[1,256]{1,0:T(1,128)} %bitcast.30, ...), custom_call_target="tpu_custom_call" | custom-call | tf_op jit(solution)/shard_map/layer_304/pallas_call | solution.py:473
  151.4 1.3 reduce_max.9
  153.4 0.0 copy-done
  153.4 0.0 copy-done.2
  153.4 0.3 conditional.1
  153.7 0.0 copy-start.1
  153.7 2.0 %copy.27 = bf16[1,128,2048]{2,1,0:T(8,128)(2,1)} copy(bf16[1,128,2048]{2,1,0:T(8,128)(2,1)} %get-tuple-element.84) | data formatting | bytes 1048576
  155.7 1.9 %copy.28 = bf16[1,128,2048]{2,1,0:T(8,128)(2,1)} copy(bf16[1,128,2048]{2,1,0:T(8,128)(2,1)} %get-tuple-element.85) | data formatting | bytes 1048576
  157.6 2.3 %copy.29 = bf16[1,512,1024]{2,1,0:T(8,128)(2,1)} copy(bf16[1,512,1024]{2,1,0:T(8,128)(2,1)} %get-tuple-element.86) | data formatting | bytes 2097152
  159.8 0.0 copy-done.1
  159.8 1.0 copy.30
Async XLA Ops:
  1.4 152.0 %copy-start = (bf16[1,128,2048]{2,1,0:T(8,128)(2,1)S(1)}, bf16[1,128,2048]{2,1,0:T(8,128)(2,1)}, u32[]{:S(2)}) copy-start(bf16[1,128,2048]{2,1,0:T(8,128)(2,1)} %param.9) | copy-start | bytes 1572868
  1.4 152.0 %copy-start.2 = (s32[1,1,256]{2,1,0:T(1,128)S(1)}, s32[1,1,256]{2,1,0:T(1,128)}, u32[]{:S(2)}) copy-start(s32[1,1,256]{2,1,0:T(1,128)} %param.11) | copy-start | bytes 3076
  153.7 6.1 %copy-start.1 = (bf16[1,1024,512]{2,1,0:T(8,128)(2,1)S(1)}, bf16[1,1024,512]{2,1,0:T(8,128)(2,1)}, u32[]{:S(2)}) copy-start(bf16[1,1024,512]{2,1,0:T(8,128)(2,1)} %get-tuple-element.87) | copy-start | bytes 3145732

commit v3 on v2

--- a/solution.py
+++ b/solution.py
@@ -443,7 +443,7 @@
         flag_copy(d).wait()
         for which in range(4):
             x_copy(which, d).wait_send()
-    flag_ref[...] = jnp.max(flags[...], axis=0)
+    flag_ref[0, 0] = jnp.max(flags[...])
     for which in range(2):
         pltpu.make_async_copy(
             final.at[which, 0], (mixed_ref, gtok_ref)[which].at[:, block(k, width)], own_sem.at[which]
@@ -477,10 +477,10 @@
             jax.ShapeDtypeStruct((tok, model), BF),
             jax.ShapeDtypeStruct((model // groups, ffw), BF),
             jax.ShapeDtypeStruct((ffw, model // groups), BF),
-            jax.ShapeDtypeStruct((PLANE, tok), I32),
+            jax.ShapeDtypeStruct((1, 1), I32),
         ),
         in_specs=[VMEM] * 4 + [pl.BlockSpec(memory_space=pl.ANY)] * 2,
-        out_specs=[VMEM] * 5,
+        out_specs=[VMEM] * 4 + [pl.BlockSpec(memory_space=pltpu.SMEM)],
         scratch_shapes=[
             pltpu.VMEM((PLANE, 1, slots), I32),
             pltpu.VMEM((planes, 2 * PLANE, tok), I32),
@@ -532,6 +532,43 @@
     )(tokens, cotangent, picks, scale, w_in, w_out)
 
 
+PIECES = 4
+
+
+def finish_kernel(count, *refs):
+    given, made, held = refs[:count], refs[count : 2 * count], refs[2 * count : 3 * count]
+    sems = refs[-1]
+
+    def copy(n, j, out):
+        rows = given[n].shape[0] // PIECES
+        part = pl.ds(j * rows, rows)
+        src, dst = (held[n], made[n]) if out else (given[n], held[n])
+        return pltpu.make_async_copy(src.at[part], dst.at[part], sems.at[int(out), n, j])
+
+    spots = [(n, j) for n in range(count) for j in range(PIECES)]
+    for n, j in spots:
+        copy(n, j, False).start()
+    for n, j in spots:
+        copy(n, j, False).wait()
+        copy(n, j, True).start()
+    for n, j in spots:
+        copy(n, j, True).wait()
+
+
+def finish(arrays):
+    anywhere = pl.BlockSpec(memory_space=pl.ANY)
+    count = len(arrays)
+    return pl.pallas_call(
+        partial(finish_kernel, count),
+        out_shape=tuple(jax.ShapeDtypeStruct(a.shape, a.dtype) for a in arrays),
+        in_specs=[anywhere] * count,
+        out_specs=[anywhere] * count,
+        scratch_shapes=[pltpu.VMEM(a.shape, a.dtype) for a in arrays]
+        + [pltpu.SemaphoreType.DMA((2, count, PIECES))],
+        name="finish",
+    )(*arrays)
+
+
 def body(tokens, cotangent, picks, valid, comb, w_in, w_out):
     planes = lax.axis_size("expert") // PLANE
     groups = lax.axis_size("dp")
@@ -541,11 +578,11 @@
     operands = (tokens[0], cotangent[0], picks[0], scale, w_in[0], w_out[0])
     results = layer(planes, groups, TIGHT, True, 0, *operands)
     results = lax.cond(
-        jnp.max(results[4]) > 0,
+        results[4][0, 0] > 0,
         lambda: tuple(layer(planes, groups, loose, False, 1, *operands)[:4]),
         lambda: tuple(results[:4]),
     )
-    return tuple(result[None] for result in results)
+    return tuple(result[None] for result in finish(results))
 
 
 def solution(mesh):

time: 162 us -> 157 us (0.969)
  local copies, waits for them, and re-layouts: 7.19 us -> 0.1 us
  Pallas kernels: 150 us -> 153 us
    unnamed x10 -> x4, local copies, waits for them, and re-layouts: 7.1 us -> 0.01 us
    pallas_call x0 -> x1, Pallas kernels: none -> 3.21 us  [finish(): pl.pallas_call(partial(finish_kernel, count), out_shape=tuple((jax.ShapeD...]
where the time goes in v3:
time: 157 us; the launch traced here: 156 us
  Pallas kernels  153 us (97%)
    pallas_call x1, Pallas kernels, layer(): pl.pallas_call(partial(layer_kernel, planes, groups, cap, stored), out_sh...  150 us
    pallas_call x1, Pallas kernels, finish(): pl.pallas_call(partial(finish_kernel, count), out_shape=tuple((jax.ShapeD...  3.21 us

profile of v3, /device:TPU:6, one launch (start us, length us, event | category | flops | bytes accessed | tf_op | source)
XLA Modules:
  0.0 155.7 jit_solution(13267059823776963818)
XLA Ops:
  0.6 0.7 convert_multiply_fusion
  1.3 0.1 broadcast_in_dim.18.scale_ref
  1.4 0.0 copy-start
  1.4 0.0 copy-start.1
  1.5 150.0 %layer_304.1 = (bf16[128,2048]{1,0:T(8,128)(2,1)}, bf16[128,2048]{1,0:T(8,128)(2,1)}, bf16[512,1024]{1,0:T(8,128)(2,1)}, bf16[1024,512]{1,0:T(8,128)(2,1)}, s32[1,1]{1,0:T(1,128)}) custom-call(bf16[128,2048]{1,0:T(8,128)(2,1)} %bitcast.15, bf16[128,2048]{1,0:T(8,128)(2,1)} %bitcast.17, s32[1,256]{1,0:T(1,128)} %bitcast.19, ...), custom_call_target="tpu_custom_call" | custom-call | tf_op jit(solution)/shard_map/layer_304/pallas_call | solution.py:473
  152.0 0.0 copy-done
  152.0 0.0 copy-done.1
  152.0 0.3 conditional.1
  152.3 3.2 %finish.1 = (bf16[128,2048]{1,0:T(8,128)(2,1)}, bf16[128,2048]{1,0:T(8,128)(2,1)}, bf16[512,1024]{1,0:T(8,128)(2,1)}, bf16[1024,512]{1,0:T(8,128)(2,1)}) custom-call(bf16[128,2048]{1,0:T(8,128)(2,1)} %get-tuple-element.52.refs_0_, bf16[128,2048]{1,0:T(8,128)(2,1)} %get-tuple-element.53.refs_1_, bf16[512,1024]{1,0:T(8,128)(2,1)} %get-tuple-element.54.refs_2_, ...), custom_call_target="tpu_custom_call" | custom-call | tf_op jit(solution)/shard_map/finish/pallas_call | solution.py:561
Async XLA Ops:
  1.4 150.6 %copy-start = (bf16[1,128,2048]{2,1,0:T(8,128)(2,1)S(1)}, bf16[1,128,2048]{2,1,0:T(8,128)(2,1)}, u32[]{:S(2)}) copy-start(bf16[1,128,2048]{2,1,0:T(8,128)(2,1)} %param.9) | copy-start | bytes 1572868
  1.4 150.5 %copy-start.1 = (s32[1,1,256]{2,1,0:T(1,128)S(1)}, s32[1,1,256]{2,1,0:T(1,128)}, u32[]{:S(2)}) copy-start(s32[1,1,256]{2,1,0:T(1,128)} %param.11) | copy-start | bytes 3076
